TPU v7x, 32 devices: a whole 2x2x4 slice. The times are simulated.
32 devices in a mesh: orbit: 2 (over x), seg: 8 (over z, y), tile: 2 (over core).
Axes of the slice: x: 2, y: 2, z: 4, core: 2. Of those that a mesh axis runs over, the one named last changes fastest.
Arguments:
- base: float32 [16, 2, 64, 4096], P(('orbit', 'seg'), None, 'tile'), parts along dimension 0, may hold values from -6 to 6
- direction: float32 [16, 2, 64, 4096], P(('orbit', 'seg'), None, 'tile'), parts along dimension 0, may hold values from -6 to 6
- step_time: float32 [2], P('orbit'), parts along dimension 0, may hold values from 0.05 to 0.15
- step_change: float32 [2], P('orbit'), parts along dimension 0, may hold values from -0.6 to 0.6
Outputs:
- grad_state: float32 [16, 2, 64, 4096], P(('orbit', 'seg'), None, 'tile'), parts along dimension 0
- grad_step: float32 [2], P('orbit'), parts along dimension 0
- residual_ms: float32 [2], P('orbit'), parts along dimension 0
There are 2 independent parts, one for each index of `orbit`. A program takes and returns all parts, laid end to end along the dimension named above; each array names one. Nothing has to cross between parts.
All inputs are finite; a program needn't handle non-finite values.
Results may differ from a plain program's by a relative error of at most 0.00002.
Values sent between devices are 32-bit elements; how exact they have to be, the bound alone decides.
A program may use at most 64 MiB of HBM per device.

v0:
```python
import math

import jax
import jax.numpy as jnp
from jax import lax
from jax.sharding import PartitionSpec as P

K_FORCE = 4


VISC = 0.5


def extended(cells, sides, width):
    for axis, dim in sides:
        count = lax.axis_size(axis)
        head = lax.slice_in_dim(cells, 0, width, axis=dim)
        tail = lax.slice_in_dim(cells, cells.shape[dim] - width, cells.shape[dim], axis=dim)
        cells = jnp.concatenate(
            [
                lax.ppermute(tail, axis, [(i, (i + 1) % count) for i in range(count)]),
                cells,
                lax.ppermute(head, axis, [((i + 1) % count, i) for i in range(count)]),
            ],
            axis=dim,
        )
    return cells


def from_behind(block, axis, distance):
    devices = range(lax.axis_size(axis))
    route = [((i - distance) % len(devices), i) for i in devices]
    return lax.ppermute(block, axis, route)


def rows_diff(wide):
    return (wide[..., 2:, :] - wide[..., :-2, :]) * 0.5


def cols_diff(inner):
    return (jnp.roll(inner, -1, -1) - jnp.roll(inner, 1, -1)) * 0.5


def laplace(wide):
    inner = wide[..., 1:-1, :]
    return (
        wide[..., 2:, :]
        + wide[..., :-2, :]
        + jnp.roll(inner, -1, -1)
        + jnp.roll(inner, 1, -1)
        - 4.0 * inner
    )


def rate(base_wide, forcing):
    inner = base_wide[:, 1:-1, :]
    value = -(inner[0] * rows_diff(base_wide) + inner[1] * cols_diff(inner)) + VISC * laplace(
        base_wide
    )
    push = jnp.stack(
        [jnp.broadcast_to(forcing, inner.shape[1:]), jnp.zeros(inner.shape[1:], jnp.float32)]
    )
    return value + push


def tangent(base_wide, pert_wide, substep):
    base_in = base_wide[:, 1:-1, :]
    pert_in = pert_wide[:, 1:-1, :]
    grad_bx = rows_diff(base_wide)
    grad_by = cols_diff(base_in)
    change = -base_in[0] * rows_diff(pert_wide) - base_in[1] * cols_diff(pert_in)
    change = change - pert_in[0] * grad_bx - pert_in[1] * grad_by + VISC * laplace(pert_wide)
    return pert_in + substep * change


def adjoint(base_wide, costate_wide, substep):
    base_in = base_wide[:, 1:-1, :]
    cost_in = costate_wide[:, 1:-1, :]
    flux_x = rows_diff(base_wide[0][None] * costate_wide)
    flux_y = cols_diff(base_in[1][None] * cost_in)
    grad_bx = rows_diff(base_wide)
    grad_by = cols_diff(base_in)
    cross = jnp.stack(
        [
            grad_bx[0] * cost_in[0] + grad_bx[1] * cost_in[1],
            grad_by[0] * cost_in[0] + grad_by[1] * cost_in[1],
        ]
    )
    return cost_in + substep * (flux_x + flux_y + VISC * laplace(costate_wide) - cross)


def extend(field):
    return extended(field, (("tile", 1),), 1)


def body(base, direction, step_time, step_change):
    substep = step_time[0]
    change = step_change[0]
    start = base[0]
    pert = direction[0]
    width = start.shape[2]
    forcing = jnp.sin(2.0 * math.pi * K_FORCE * jnp.arange(width, dtype=jnp.float32) / width)
    first_wide = extend(jnp.concatenate([start, pert], axis=0))
    start_wide = first_wide[:2]
    rate_zero = rate(start_wide, forcing)
    middle = start + substep * rate_zero
    pert_one = tangent(start_wide, first_wide[2:], substep) + change * rate_zero
    second_wide = extend(jnp.concatenate([middle, pert_one], axis=0))
    middle_wide = second_wide[:2]
    rate_one = rate(middle_wide, forcing)
    image = tangent(middle_wide, second_wide[2:], substep) + change * rate_one
    carried = from_behind(image, "seg", 1)
    behind = carried - pert
    resid = from_behind(behind, "seg", -1)
    local_square = jnp.sum(resid * resid)
    total_square = lax.psum(local_square, ("seg", "tile"))
    adj_one = adjoint(middle_wide, extend(resid), substep)
    adj_zero = adjoint(start_wide, extend(adj_one), substep)
    grad_state = adj_zero - behind
    local_time = jnp.sum(rate_zero * adj_one) + jnp.sum(rate_one * resid)
    total_time = lax.psum(local_time, ("seg", "tile"))
    cells = start.shape[1] * width * lax.axis_size("seg") * lax.axis_size("tile")
    grad_step = (total_time / cells).reshape(1)
    residual_ms = (total_square / (2 * cells)).reshape(1)
    return (grad_state[None], grad_step, residual_ms)


def solution(mesh):
    in_specs = (
        P(("orbit", "seg"), None, "tile", None),
        P(("orbit", "seg"), None, "tile", None),
        P("orbit"),
        P("orbit"),
    )
    out_specs = (P(("orbit", "seg"), None, "tile", None), P("orbit"), P("orbit"))
    return jax.shard_map(body, mesh=mesh, in_specs=in_specs, out_specs=out_specs, check_vma=False)
```

profile of v0, /device:TPU:0, one launch (start us, length us, event | category | flops | bytes accessed | tf_op | source)
XLA Modules:
  0.0 122.0 jit_solution(6295365935500278912)
XLA Ops:
  0.6 0.0 copy-start.1
  0.6 0.0 copy-start
  0.6 1.4 %pad_maximum_fusion.32 = (f32[4,1,4096]{2,1,0:T(1,128)S(1)}, f32[4,1,4096]{2,1,0:T(1,128)S(1)}) fusion(f32[2,32,4096]{2,1,0:T(8,128)} %bitcast.51, f32[2,32,4096]{2,1,0:T(8,128)} %bitcast.45), kind=kLoop, calls=%fused_computation.106 | loop fusion | flops 32768 | bytes 2228224 | tf_op jit(solution)/shard_map/concatenate | solution.py:103
  2.1 0.5 collective-permute-start
  2.6 0.1 collective-permute-start.1
  2.7 0.7 fusion.49
  3.4 0.1 fusion.50
  3.5 0.3 multiply_bitcast_fusion.4
  5.1 0.1 multiply_sine_fusion
  5.2 0.0 collective-permute-done
  5.2 0.0 collective-permute-done.1
  5.3 2.7 %multiply_add_fusion.2 = (f32[2,32,4096]{2,1,0:T(8,128)S(1)}, f32[2,32,4096]{2,1,0:T(8,128)S(1)}) fusion(f32[2,32,4096]{2,1,0:T(8,128)S(1)} %bitcast.54, f32[2,32,4095]{2,1,0:T(8,128)S(1)} %get-tuple-element.71, f32[2,32,1]{2,1,0:T(8,128)S(1)} %get-tuple-element.73, f32[2,32,1]{2,1,0:T(8,128)S(1)} %get-tuple-element.74, ...), kind=kLoop, calls=%fused_computation.59 | loop fusion | flops 12058624 | bytes 11665416 | tf_op jit(solution)/shard_map/add | solution.py:107
  7.9 0.3 fusion.47
  8.3 0.1 fusion.48
  8.4 0.1 fusion.31
  8.5 0.1 multiply_add_fusion.1
  8.6 0.1 pad_maximum_fusion.30
  8.7 0.1 slice_bitcast_fusion
  8.8 0.3 fusion.45
  9.2 0.5 collective-permute-start.2
  9.7 0.1 collective-permute-start.3
  9.8 0.1 fusion.46
  9.8 0.7 collective-permute-done.2
  10.6 0.4 collective-permute-done.3
  10.9 2.6 %multiply_add_fusion = (f32[2,32,4096]{2,1,0:T(8,128)S(1)}, f32[2,32,4096]{2,1,0:T(8,128)S(1)}) fusion(f32[2,32,4096]{2,1,0:T(8,128)S(1)} %get-tuple-element.11, f32[2,32,4095]{2,1,0:T(8,128)S(1)} %get-tuple-element.55, f32[2,32,1]{2,1,0:T(8,128)S(1)} %get-tuple-element.57, f32[2,32,1]{2,1,0:T(8,128)S(1)} %get-tuple-element.56, ...), kind=kLoop, calls=%fused_computation.57 | loop fusion | flops 12058624 | bytes 11665416 | tf_op jit(solution)/shard_map/add | solution.py:111
  13.6 2.7 %collective-permute-start.4 = (f32[2,32,4096]{2,1,0:T(8,128)S(1)}, f32[2,32,4096]{2,1,0:T(8,128)S(1)}, u32[]{:S(2)}, u32[]{:S(2)}) collective-permute-start(f32[2,32,4096]{2,1,0:T(8,128)S(1)} %get-tuple-element.9), channel_id=1, source_target_pairs={{14,0},{0,2},{2,4},{4,6},{6,8},{8,10},{10,12},{12,14},{15,1},{1,3}... | collective-permute-start | bytes 3145736 | tf_op jit(solution)/shard_map/ppermute | solution.py:33
  16.3 0.3 broadcast_multiply_fusion.2
  16.6 0.3 broadcast_multiply_fusion.4
  17.0 0.3 broadcast_multiply_fusion.3
  17.3 25.7 %collective-permute-done.4 = f32[2,32,4096]{2,1,0:T(8,128)S(1)} collective-permute-done((f32[2,32,4096]{2,1,0:T(8,128)S(1)}, f32[2,32,4096]{2,1,0:T(8,128)S(1)}, u32[]{:S(2)}, u32[]{:S(2)}) %collective-permute-start.4) | collective-permute-done | bytes 1048608 | tf_op jit(solution)/shard_map/ppermute | solution.py:33
  43.0 0.1 bitcast_subtract_fusion
  43.1 1.8 %collective-permute-start.5 = (f32[2,32,4096]{2,1,0:T(8,128)S(1)}, f32[2,32,4096]{2,1,0:T(8,128)S(1)}, u32[]{:S(2)}, u32[]{:S(2)}) collective-permute-start(f32[2,32,4096]{2,1,0:T(8,128)S(1)} %bitcast_subtract_fusion), channel_id=1, source_target_pairs={{2,0},{4,2},{6,4},{8,6},{10,8},{12,10},{14,12},{0,14},{3,1},{5,3},... | collective-permute-start | bytes 3145736 | tf_op jit(solution)/shard_map/ppermute | solution.py:33
  44.9 0.9 fusion.24
  45.8 0.1 fusion.25
  45.9 0.3 broadcast_multiply_fusion.5
  46.2 21.8 %collective-permute-done.5 = f32[2,32,4096]{2,1,0:T(8,128)S(1)} collective-permute-done((f32[2,32,4096]{2,1,0:T(8,128)S(1)}, f32[2,32,4096]{2,1,0:T(8,128)S(1)}, u32[]{:S(2)}, u32[]{:S(2)}) %collective-permute-start.5) | collective-permute-done | bytes 1048608 | tf_op jit(solution)/shard_map/ppermute | solution.py:33
  68.0 0.9 multiply_reduce_fusion
  68.9 0.3 fusion.40
  69.3 0.1 fusion.41
  69.4 0.1 collective-permute-start.6
  69.5 0.5 collective-permute-start.7
  70.0 0.3 fusion.43
  70.3 0.2 fusion.29
  70.5 0.1 fusion.44
  70.6 0.1 collective-permute-done.6
  70.7 0.2 collective-permute-done.7
  70.8 0.2 maximum_multiply_fusion
  71.0 1.7 %multiply_reduce_fusion.2 = (f32[]{:T(128)}, f32[2,32,4096]{2,1,0:T(8,128)S(1)}) fusion(f32[2,32,4096]{2,1,0:T(8,128)S(1)} %get-tuple-element.12, f32[2,32,4096]{2,1,0:T(8,128)S(1)} %collective-permute-done.5, f32[1,32,4096]{2,1,0:T(8,128)S(1)} %get-tuple-element.47, f32[1,32,4096]{2,1,0:T(8,128)S(1)} %get-tuple-element.46, ...), kind=kLoop, calls=%fused_computation.56 | loop fusion | flops 5767167 | bytes 10551304 | tf_op jit(solution)/shard_map/reduce_sum | solution.py:120
  72.7 0.1 broadcast_multiply_fusion
  72.8 0.1 fusion.37
  72.9 1.3 %fusion.38 = (f32[2,32,4095]{2,1,0:T(8,128)S(1)}, f32[2,32,4095]{2,1,0:T(8,128)}) fusion(f32[2,32,4096]{2,1,0:T(8,128)S(1)} %broadcast_multiply_fusion), kind=kLoop, calls=%fused_computation.113 | loop fusion | bytes 4193280 | tf_op jit(solution)/shard_map/jit(_roll_static)/slice | solution.py:41
  74.2 1.7 %fusion.36 = (f32[2,32,4095]{2,1,0:T(8,128)}, f32[2,32,4095]{2,1,0:T(8,128)}) fusion(f32[2,32,4096]{2,1,0:T(8,128)S(1)} %get-tuple-element.8), kind=kLoop, calls=%fused_computation.111 | loop fusion | bytes 4193280 | tf_op jit(solution)/shard_map/jit(_roll_static)/slice | solution.py:50
  75.9 0.3 collective-permute-start.8
  76.2 0.2 collective-permute-start.9
  76.4 1.2 fusion.27
  77.6 0.1 fusion.35
  78.9 34.3 %all-reduce.1 = (f32[]{:T(128)}, f32[]{:T(128)}) all-reduce(f32[]{:T(128)S(6)} %add.181, f32[]{:T(128)} %get-tuple-element.3), channel_id=1, replica_groups=mesh['orbit'=2,'seg'=8,'tile'=2] {'seg','tile'}, use_global_device_ids=true, to_apply=%region_2.3 | all-reduce | flops 2 | bytes 16 | tf_op jit(solution)/shard_map/psum | solution.py:121
  114.5 0.0 copy-start.2
  114.5 0.0 collective-permute-done.8
  114.5 0.0 collective-permute-done.9
  114.6 1.4 %maximum_multiply_fusion.1 = f32[2,34,4096]{2,1,0:T(8,128)S(1)} fusion(f32[2,1,4096]{2,1,0:T(1,128)S(1)} %collective-permute-done.9, f32[2,32,4096]{2,1,0:T(8,128)S(1)} %get-tuple-element.8, f32[2,1,4096]{2,1,0:T(1,128)S(1)} %collective-permute-done.8, f32[34,4096]{1,0:T(8,128)} %fusion.24), kind=kLoop, calls=%fused_computation.3 | loop fusion | flops 835584 | bytes 2785280 | tf_op jit(solution)/shard_map/mul | solution.py:79
  116.0 0.3 copy-done.3
  116.2 0.1 copy-done.4
  116.4 3.4 %fusion.10 = f32[1,2,32,4096]{3,2,1,0:T(8,128)} fusion(f32[2,32,4096]{2,1,0:T(8,128)S(1)} %bitcast_subtract_fusion, f32[2,32,4096]{2,1,0:T(8,128)S(1)} %get-tuple-element.8, f32[2,1,4096]{2,1,0:T(1,128)S(1)} %collective-permute-done.8, f32[2,1,4096]{2,1,0:T(1,128)S(1)} %collective-permute-done.9, f32[2,34,4096]{2,1,0:T(8,128)S(1)} %maximum_multiply_fusion.1, ...), kind=kLoop, calls=%fused_computation.15 | loop fusion | flops 5505024 | bytes 10551300 | tf_op jit(solution)/shard_map/broadcast_in_dim | solution.py:125
  (10 shorter events, 0.2 us)
Async XLA Ops:
  0.6 2.0 %copy-start.1 = (f32[1,2,32,4096]{3,2,1,0:T(8,128)S(1)}, f32[1,2,32,4096]{3,2,1,0:T(8,128)}, u32[]{:S(2)}) copy-start(f32[1,2,32,4096]{3,2,1,0:T(8,128)} %param.5) | copy-start | bytes 3145732
  0.6 2.0 %copy-start = (f32[1,2,32,4096]{3,2,1,0:T(8,128)S(1)}, f32[1,2,32,4096]{3,2,1,0:T(8,128)}, u32[]{:S(2)}) copy-start(f32[1,2,32,4096]{3,2,1,0:T(8,128)} %param.4) | copy-start | bytes 3145732
  2.1 3.1 %collective-permute-start = (f32[4,1,4096]{2,1,0:T(1,128)S(1)}, f32[4,1,4096]{2,1,0:T(1,128)S(1)}, u32[]{:S(2)}, u32[]{:S(2)}) collective-permute-start(f32[4,1,4096]{2,1,0:T(1,128)S(1)} %get-tuple-element.16), channel_id=1, source_target_pairs={{1,0},{0,1},{3,2},{2,3},{5,4},{4,5},{7,6},{6,7},{9,8},{8,9},{11,10... | collective-permute-start | bytes 196616 | tf_op jit(solution)/shard_map/ppermute | solution.py:23
  2.6 2.6 %collective-permute-start.1 = (f32[4,1,4096]{2,1,0:T(1,128)S(1)}, f32[4,1,4096]{2,1,0:T(1,128)S(1)}, u32[]{:S(2)}, u32[]{:S(2)}) collective-permute-start(f32[4,1,4096]{2,1,0:T(1,128)S(1)} %get-tuple-element.15), channel_id=1, source_target_pairs={{0,1},{1,0},{2,3},{3,2},{4,5},{5,4},{6,7},{7,6},{8,9},{9,8},{10,11... | collective-permute-start | bytes 196616 | tf_op jit(solution)/shard_map/ppermute | solution.py:21
  9.2 1.4 %collective-permute-start.2 = (f32[4,1,4096]{2,1,0:T(1,128)S(1)}, f32[4,1,4096]{2,1,0:T(1,128)S(1)}, u32[]{:S(2)}, u32[]{:S(2)}) collective-permute-start(f32[4,1,4096]{2,1,0:T(1,128)S(1)} %get-tuple-element.14), channel_id=1, source_target_pairs={{1,0},{0,1},{3,2},{2,3},{5,4},{4,5},{7,6},{6,7},{9,8},{8,9},{11,10... | collective-permute-start | bytes 196616 | tf_op jit(solution)/shard_map/ppermute | solution.py:23
  9.7 1.3 %collective-permute-start.3 = (f32[4,1,4096]{2,1,0:T(1,128)S(1)}, f32[4,1,4096]{2,1,0:T(1,128)S(1)}, u32[]{:S(2)}, u32[]{:S(2)}) collective-permute-start(f32[4,1,4096]{2,1,0:T(1,128)S(1)} %get-tuple-element.13), channel_id=1, source_target_pairs={{0,1},{1,0},{2,3},{3,2},{4,5},{5,4},{6,7},{7,6},{8,9},{9,8},{10,11... | collective-permute-start | bytes 196616 | tf_op jit(solution)/shard_map/ppermute | solution.py:21
  13.6 29.4 %collective-permute-start.4 = (f32[2,32,4096]{2,1,0:T(8,128)S(1)}, f32[2,32,4096]{2,1,0:T(8,128)S(1)}, u32[]{:S(2)}, u32[]{:S(2)}) collective-permute-start(f32[2,32,4096]{2,1,0:T(8,128)S(1)} %get-tuple-element.9), channel_id=1, source_target_pairs={{14,0},{0,2},{2,4},{4,6},{6,8},{8,10},{10,12},{12,14},{15,1},{1,3}... | collective-permute-start | bytes 3145736 | tf_op jit(solution)/shard_map/ppermute | solution.py:33
  43.1 24.9 %collective-permute-start.5 = (f32[2,32,4096]{2,1,0:T(8,128)S(1)}, f32[2,32,4096]{2,1,0:T(8,128)S(1)}, u32[]{:S(2)}, u32[]{:S(2)}) collective-permute-start(f32[2,32,4096]{2,1,0:T(8,128)S(1)} %bitcast_subtract_fusion), channel_id=1, source_target_pairs={{2,0},{4,2},{6,4},{8,6},{10,8},{12,10},{14,12},{0,14},{3,1},{5,3},... | collective-permute-start | bytes 3145736 | tf_op jit(solution)/shard_map/ppermute | solution.py:33
  69.4 1.3 %collective-permute-start.6 = (f32[2,1,4096]{2,1,0:T(1,128)S(1)}, f32[2,1,4096]{2,1,0:T(1,128)S(1)}, u32[]{:S(2)}, u32[]{:S(2)}) collective-permute-start(f32[2,1,4096]{2,1,0:T(1,128)S(1)} %get-tuple-element.41), channel_id=1, source_target_pairs={{0,1},{1,0},{2,3},{3,2},{4,5},{5,4},{6,7},{7,6},{8,9},{9,8},{10,11... | collective-permute-start | bytes 98312 | tf_op jit(solution)/shard_map/ppermute | solution.py:21
  69.5 1.4 %collective-permute-start.7 = (f32[2,1,4096]{2,1,0:T(1,128)S(1)}, f32[2,1,4096]{2,1,0:T(1,128)S(1)}, u32[]{:S(2)}, u32[]{:S(2)}) collective-permute-start(f32[2,1,4096]{2,1,0:T(1,128)S(1)} %get-tuple-element.40), channel_id=1, source_target_pairs={{1,0},{0,1},{3,2},{2,3},{5,4},{4,5},{7,6},{6,7},{9,8},{8,9},{11,10... | collective-permute-start | bytes 98312 | tf_op jit(solution)/shard_map/ppermute | solution.py:23
  75.9 38.7 %collective-permute-start.8 = (f32[2,1,4096]{2,1,0:T(1,128)S(1)}, f32[2,1,4096]{2,1,0:T(1,128)S(1)}, u32[]{:S(2)}, u32[]{:S(2)}) collective-permute-start(f32[2,1,4096]{2,1,0:T(1,128)S(1)} %get-tuple-element.32), channel_id=1, source_target_pairs={{0,1},{1,0},{2,3},{3,2},{4,5},{5,4},{6,7},{7,6},{8,9},{9,8},{10,11... | collective-permute-start | bytes 98312 | tf_op jit(solution)/shard_map/ppermute | solution.py:21
  76.2 38.3 %collective-permute-start.9 = (f32[2,1,4096]{2,1,0:T(1,128)S(1)}, f32[2,1,4096]{2,1,0:T(1,128)S(1)}, u32[]{:S(2)}, u32[]{:S(2)}) collective-permute-start(f32[2,1,4096]{2,1,0:T(1,128)S(1)} %get-tuple-element.31), channel_id=1, source_target_pairs={{1,0},{0,1},{3,2},{2,3},{5,4},{4,5},{7,6},{6,7},{9,8},{8,9},{11,10... | collective-permute-start | bytes 98312 | tf_op jit(solution)/shard_map/ppermute | solution.py:23
  114.5 1.5 %copy-start.2 = (f32[2,32,4095]{2,1,0:T(8,128)S(1)}, f32[2,32,4095]{2,1,0:T(8,128)}, u32[]{:S(2)}) copy-start(f32[2,32,4095]{2,1,0:T(8,128)} %get-tuple-element.27) | copy-start | bytes 3144964
  114.5 1.7 %copy-start.3 = (f32[2,32,4095]{2,1,0:T(8,128)S(1)}, f32[2,32,4095]{2,1,0:T(8,128)}, u32[]{:S(2)}) copy-start(f32[2,32,4095]{2,1,0:T(8,128)} %get-tuple-element.22) | copy-start | bytes 3144964
  114.5 1.9 %copy-start.4 = (f32[1,32,4096]{2,1,0:T(8,128)S(1)}, f32[1,32,4096]{2,1,0:T(8,128)}, u32[]{:S(2)}) copy-start(f32[1,32,4096]{2,1,0:T(8,128)} %get-tuple-element.18) | copy-start | bytes 1572868
where the time goes:
time: 122 us
  waiting for transfers between devices  49 us (40%)
  blocking collectives  34.3 us (28%)
  other arithmetic  18.8 us (15%)
  between operations  7.03 us (6%)
  starting transfers between devices  6.77 us (6%)
  local copies, waits for them, and re-layouts  6.16 us (5%)
    ppermute x2, waiting for transfers between devices, from_behind(): return lax.ppermute(block, axis, route)  47.6 us
    psum x1, blocking collectives, body(): total_time = lax.psum(local_time, ('seg', 'tile'))  34.3 us
    ppermute x2, starting transfers between devices, from_behind(): return lax.ppermute(block, axis, route)  4.52 us
    slice x10, local copies, waits for them, and re-layouts, cols_diff(): return (jnp.roll(inner, -1, -1) - jnp.roll(inner, 1, -1)) * 0.5  3.48 us
    broadcast_in_dim x1, other arithmetic, body(): return (grad_state[None], grad_step, residual_ms)  3.39 us
    add x1, other arithmetic, body(): pert_one = tangent(start_wide, first_wide[2:], substep) + change * rate_zero  2.66 us
    add x1, other arithmetic, body(): image = tangent(middle_wide, second_wide[2:], substep) + change * rate_one  2.62 us
    mul x4, other arithmetic, adjoint(): flux_x = rows_diff(base_wide[0][None] * costate_wide)  2.59 us
  transfers between devices with their start and end apart: 10, of which 6 were waited for; matrix products, arithmetic and copies ran while one was open for 4% of the time, Pallas kernels for 0%

commit v1 on v0

v1 whole, which is shorter than its diff:
```python
import functools
import math

import jax
import jax.numpy as jnp
import numpy as np
from jax import lax
from jax.experimental import pallas as pl
from jax.experimental.pallas import tpu as pltpu
from jax.sharding import PartitionSpec as P

K_FORCE = 4

VISC = 0.5

MESH = pl.DeviceIdType.MESH
LANES = 128
SUB = 8
CHUNK = 256


class Window:
    def __init__(self, ref, comp, col, width):
        full, rows = ref.shape[-1], ref.shape[-2] - 2 * SUB
        here = pl.ds(pl.multiple_of(col, LANES), width)
        before = pl.multiple_of(lax.rem(col + (full - LANES), full), LANES)
        after = pl.multiple_of(lax.rem(col + width, full), LANES)
        own = pl.ds(SUB, rows)
        self.mid = ref[comp, own, here]
        self.up = ref[comp, pl.ds(SUB - 1, rows), here]
        self.down = ref[comp, pl.ds(SUB + 1, rows), here]
        wide = jnp.concatenate(
            [ref[comp, own, pl.ds(before, LANES)], self.mid, ref[comp, own, pl.ds(after, LANES)]], axis=1
        )
        self.left = pltpu.roll(wide, 1, 1)[:, LANES : LANES + width]
        self.right = pltpu.roll(wide, wide.shape[1] - 1, 1)[:, LANES : LANES + width]

    def dx(self):
        return (self.down - self.up) * 0.5

    def dy(self):
        return (self.right - self.left) * 0.5

    def lap(self):
        return self.down + self.up + self.right + self.left - 4.0 * self.mid


def windows(ref, col, width):
    return Window(ref, 0, col, width), Window(ref, 1, col, width)


def rate_and_tangent(b, p, forcing, substep, change):
    rates, images = [], []
    for c in range(2):
        gx, gy = b[c].dx(), b[c].dy()
        rate = -(b[0].mid * gx + b[1].mid * gy) + VISC * b[c].lap()
        if c == 0:
            rate = rate + forcing
        move = -b[0].mid * p[c].dx() - b[1].mid * p[c].dy() - p[0].mid * gx - p[1].mid * gy
        move = move + VISC * p[c].lap()
        rates.append(rate)
        images.append(p[c].mid + substep * move + change * rate)
    return rates, images


def adjoint(b, q, substep):
    outs = []
    for c in range(2):
        flux_x = (b[0].down * q[c].down - b[0].up * q[c].up) * 0.5
        flux_y = (b[1].right * q[c].right - b[1].left * q[c].left) * 0.5
        if c == 0:
            cross = b[0].dx() * q[0].mid + b[1].dx() * q[1].mid
        else:
            cross = b[0].dy() * q[0].mid + b[1].dy() * q[1].mid
        outs.append(q[c].mid + substep * (flux_x + flux_y + VISC * q[c].lap() - cross))
    return outs


def folded(x):
    total = None
    for i in range(x.shape[0] // SUB):
        for k in range(x.shape[1] // LANES):
            part = x[i * SUB : (i + 1) * SUB, k * LANES : (k + 1) * LANES]
            total = part if total is None else total + part
    return total


def kernel(
    n_seg, n_tile, scale_time, scale_square,
    base_hbm, pert_hbm, time_ref, change_ref, force_ref,
    grad_ref, step_ref, square_ref,
    base, pert, mid, pone, res, adj, rate0, rate1, image, ahead, behind, sums, pair, slots,
    local_sem, edge_send, edge_recv, ahead_send, ahead_recv, behind_send, behind_recv,
    pair_sem, slot_send, slot_recv,
):
    seg = lax.axis_index("seg")
    tile = lax.axis_index("tile")
    seg_next, seg_prev = lax.rem(seg + 1, n_seg), lax.rem(seg + n_seg - 1, n_seg)
    tile_next, tile_prev = lax.rem(tile + 1, n_tile), lax.rem(tile + n_tile - 1, n_tile)
    rows, width = pert_hbm.shape[2], pert_hbm.shape[3]
    blocks = rows // SUB
    chunk = min(CHUNK, width)
    substep, change = time_ref[0], change_ref[0]

    barrier = pltpu.get_barrier_semaphore()
    for k in range(1, n_seg):
        pl.semaphore_signal(barrier, inc=1, device_id={"seg": lax.rem(seg + k, n_seg)}, device_id_type=MESH)
    for k in range(1, n_tile):
        pl.semaphore_signal(barrier, inc=1, device_id={"tile": lax.rem(tile + k, n_tile)}, device_id_type=MESH)

    own = pl.ds(SUB, rows)
    loads = [
        pltpu.make_async_copy(base_hbm.at[0], base.at[:, own, :], local_sem.at[0]),
        pltpu.make_async_copy(pert_hbm.at[0], pert.at[:, own, :], local_sem.at[1]),
    ]
    for copy in loads:
        copy.start()
    pl.semaphore_wait(barrier, n_seg - 1 + n_tile - 1)

    def edges(first, last, field, at):
        down = pltpu.make_async_remote_copy(
            src_ref=last, dst_ref=field.at[:, pl.ds(0, SUB), :], send_sem=edge_send.at[at], recv_sem=edge_recv.at[at],
            device_id={"tile": tile_next}, device_id_type=MESH)
        up = pltpu.make_async_remote_copy(
            src_ref=first, dst_ref=field.at[:, pl.ds(SUB + rows, SUB), :], send_sem=edge_send.at[at + 1],
            recv_sem=edge_recv.at[at + 1], device_id={"tile": tile_prev}, device_id_type=MESH)
        down.start()
        up.start()
        return [down, up]

    def field_edges(field, at):
        return edges(field.at[:, pl.ds(SUB, SUB), :], field.at[:, pl.ds(rows, SUB), :], field, at)

    def hbm_edges(field_hbm, field, at):
        return edges(field_hbm.at[0, :, pl.ds(0, SUB), :], field_hbm.at[0, :, pl.ds(rows - SUB, SUB), :], field, at)

    pending = hbm_edges(base_hbm, base, 0) + hbm_edges(pert_hbm, pert, 2)
    aheads = []
    for k in range(blocks):
        part = pl.ds(k * SUB, SUB)
        copy = pltpu.make_async_remote_copy(
            src_ref=pert_hbm.at[0, :, part, :], dst_ref=ahead.at[:, part, :], send_sem=ahead_send.at[k],
            recv_sem=ahead_recv.at[k], device_id={"seg": seg_prev}, device_id_type=MESH)
        copy.start()
        aheads.append(copy)

    def sweep(step):
        def one(j, _):
            step(pl.multiple_of(j * chunk, chunk))
            return 0

        lax.fori_loop(0, width // chunk, one, 0)

    sums[...] = jnp.zeros_like(sums)
    for copy in loads:
        copy.wait()
    for copy in pending:
        copy.wait()

    def first_step(col):
        b, p = windows(base, col, chunk), windows(pert, col, chunk)
        forcing = force_ref[:, pl.ds(col, chunk)]
        rates, images = rate_and_tangent(b, p, forcing, substep, change)
        for c in range(2):
            rate0[c, :, pl.ds(col, chunk)] = rates[c]
            mid[c, own, pl.ds(col, chunk)] = b[c].mid + substep * rates[c]
            pone[c, own, pl.ds(col, chunk)] = images[c]

    sweep(first_step)
    for copy in field_edges(mid, 4) + field_edges(pone, 6):
        copy.wait()

    def second_step(col):
        b, p = windows(mid, col, chunk), windows(pone, col, chunk)
        forcing = force_ref[:, pl.ds(col, chunk)]
        rates, images = rate_and_tangent(b, p, forcing, substep, change)
        for c in range(2):
            rate1[c, :, pl.ds(col, chunk)] = rates[c]
            image[c, :, pl.ds(col, chunk)] = images[c]

    sweep(second_step)
    for copy in aheads:
        copy.wait_send()
    behinds = []
    for k in range(blocks):
        part = pl.ds(k * SUB, SUB)
        copy = pltpu.make_async_remote_copy(
            src_ref=image.at[:, part, :], dst_ref=behind.at[:, part, :], send_sem=behind_send.at[k],
            recv_sem=behind_recv.at[k], device_id={"seg": seg_next}, device_id_type=MESH)
        copy.start()
        behinds.append(copy)

    for k in range(blocks):
        aheads[k].wait_recv()
        part, wide_part = pl.ds(k * SUB, SUB), pl.ds((k + 1) * SUB, SUB)

        def residual_step(col):
            for c in range(2):
                value = image[c, part, pl.ds(col, chunk)] - ahead[c, part, pl.ds(col, chunk)]
                res[c, wide_part, pl.ds(col, chunk)] = value
                sums[0] += folded(value * value)
                sums[1] += folded(rate1[c, part, pl.ds(col, chunk)] * value)

        sweep(residual_step)
    for copy in field_edges(res, 8):
        copy.wait()

    def adjoint_one(col):
        outs = adjoint(windows(mid, col, chunk), windows(res, col, chunk), substep)
        for c in range(2):
            adj[c, own, pl.ds(col, chunk)] = outs[c]
            sums[1] += folded(rate0[c, :, pl.ds(col, chunk)] * outs[c])

    sweep(adjoint_one)
    pending = field_edges(adj, 10)
    shares = []
    for k in range(1, n_tile):
        copy = pltpu.make_async_remote_copy(
            src_ref=sums, dst_ref=pair.at[tile], send_sem=pair_sem.at[0, k], recv_sem=pair_sem.at[1, tile],
            device_id={"tile": lax.rem(tile + k, n_tile)}, device_id_type=MESH)
        copy.start()
        shares.append(copy)
    for copy in pending:
        copy.wait()

    def adjoint_zero(col):
        outs = adjoint(windows(base, col, chunk), windows(adj, col, chunk), substep)
        for c in range(2):
            pone[c, own, pl.ds(col, chunk)] = outs[c] + pert[c, own, pl.ds(col, chunk)]

    sweep(adjoint_zero)

    for copy in shares:
        copy.wait_send()
    for k in range(1, n_tile):
        source = lax.rem(tile + k, n_tile)
        pltpu.make_async_remote_copy(
            src_ref=sums, dst_ref=pair.at[source], send_sem=pair_sem.at[0, k], recv_sem=pair_sem.at[1, source],
            device_id={"tile": source}, device_id_type=MESH).wait_recv()
    pair[tile] = sums[...]
    both = pair[0]
    for k in range(1, n_tile):
        both = both + pair[k]
    slots[seg] = both
    sends = []
    for k in range(1, n_seg):
        copy = pltpu.make_async_remote_copy(
            src_ref=slots.at[seg], dst_ref=slots.at[seg], send_sem=slot_send.at[k], recv_sem=slot_recv.at[seg],
            device_id={"seg": lax.rem(seg + k, n_seg)}, device_id_type=MESH)
        copy.start()
        sends.append(copy)
    for copy in sends:
        copy.wait_send()
    for k in range(1, n_seg):
        source = lax.rem(seg + k, n_seg)
        pltpu.make_async_remote_copy(
            src_ref=slots.at[source], dst_ref=slots.at[source], send_sem=slot_send.at[k],
            recv_sem=slot_recv.at[source], device_id={"seg": source}, device_id_type=MESH).wait_recv()
    total = slots[0]
    for k in range(1, n_seg):
        total = total + slots[k]
    square_ref[0] = jnp.sum(total[0]) * scale_square
    step_ref[0] = jnp.sum(total[1]) * scale_time

    for k in range(blocks):
        behinds[k].wait_recv()
        part, wide_part = pl.ds(k * SUB, SUB), pl.ds((k + 1) * SUB, SUB)

        def last_step(col):
            for c in range(2):
                here = pl.ds(col, chunk)
                grad_ref[0, c, part, here] = pone[c, wide_part, here] - behind[c, part, here]

        sweep(last_step)
    for copy in behinds:
        copy.wait_send()


def body(n_seg, n_tile, base, direction, step_time, step_change):
    _, comps, rows, width = base.shape
    cells = rows * width * n_seg * n_tile
    forcing = np.sin(2.0 * math.pi * K_FORCE * np.arange(width) / width).astype(np.float32)[None]
    blocks = rows // SUB
    wide = pltpu.VMEM((comps, rows + 2 * SUB, width), jnp.float32)
    plain = pltpu.VMEM((comps, rows, width), jnp.float32)
    part = (2, SUB, LANES)
    dma = pltpu.SemaphoreType.DMA
    anywhere = pl.BlockSpec(memory_space=pl.ANY)
    scalar = pl.BlockSpec(memory_space=pltpu.SMEM)
    vector = pl.BlockSpec(memory_space=pltpu.VMEM)
    one = jax.ShapeDtypeStruct((1,), jnp.float32)
    return pl.pallas_call(
        functools.partial(kernel, n_seg, n_tile, 1.0 / cells, 1.0 / (2 * cells)),
        out_shape=(jax.ShapeDtypeStruct(base.shape, jnp.float32), one, one),
        in_specs=[anywhere, anywhere, scalar, scalar, vector],
        out_specs=(vector, scalar, scalar),
        scratch_shapes=[wide] * 6 + [plain] * 5 + [
            pltpu.VMEM(part, jnp.float32),
            pltpu.VMEM((n_tile, *part), jnp.float32),
            pltpu.VMEM((n_seg, *part), jnp.float32),
            dma((2,)), dma((12,)), dma((12,)), dma((blocks,)), dma((blocks,)), dma((blocks,)), dma((blocks,)),
            dma((2, n_tile)), dma((n_seg,)), dma((n_seg,)),
        ],
        compiler_params=pltpu.CompilerParams(
            collective_id=0, has_side_effects=True, vmem_limit_bytes=40 * 1024 * 1024
        ),
    )(base, direction, step_time, step_change, forcing)


def solution(mesh):
    spec = P(("orbit", "seg"), None, "tile", None)
    return jax.shard_map(
        functools.partial(body, mesh.shape["seg"], mesh.shape["tile"]),
        mesh=mesh,
        in_specs=(spec, spec, P("orbit"), P("orbit")),
        out_specs=(spec, P("orbit"), P("orbit")),
        check_vma=False,
    )
```

time: 122 us -> 74.3 us (0.61)
  Pallas kernels: 0 us -> 64.5 us
  waiting for transfers between devices: 49 us -> 0 us
  blocking collectives: 34.3 us -> 0 us
  other arithmetic: 18.8 us -> 0 us
  starting transfers between devices: 6.77 us -> 0 us
  local copies, waits for them, and re-layouts: 6.16 us -> 4.13 us
  between operations: 7.03 us -> 5.42 us
    pallas_call x0 -> x1, Pallas kernels: none -> 64.5 us  [body(): pl.pallas_call(functools.partial(kernel, n_seg, n_tile, 1.0 / cells, 1.0...]
    ppermute x10 -> x0, waiting for transfers between devices: 49 us -> none  [the longest x2 47.6 us: from_behind(): return lax.ppermute(block, axis, route)]
    psum x1 -> x0, blocking collectives: 34.3 us -> none  [body(): total_time = lax.psum(local_time, ('seg', 'tile'))]
    ppermute x10 -> x0, starting transfers between devices: 6.77 us -> none  [the longest x2 4.52 us: from_behind(): return lax.ppermute(block, axis, route)]
    add x5 -> x0, other arithmetic: 6.7 us -> none  [the longest x1 2.66 us: body(): pert_one = tangent(start_wide, first_wide[2:], substep) + change * rate_zero]
    slice x16 -> x0, local copies, waits for them, and re-layouts: 5.72 us -> none  [the longest x10 3.48 us: cols_diff(): return (jnp.roll(inner, -1, -1) - jnp.roll(inner, 1, -1)) * 0.5]
    mul x14 -> x0, other arithmetic: 4.48 us -> none  [the longest x4 2.59 us: adjoint(): flux_x = rows_diff(base_wide[0][None] * costate_wide)]
    unnamed x10 -> x7, local copies, waits for them, and re-layouts: 0.4 us -> 4.13 us
  transfers between devices with their start and end apart: 10 -> 0, of which waited for: 6 -> 0; matrix products, arithmetic and copies ran while one was open for 4% -> 0% of each run, Pallas kernels for 0% -> 0%
where the time goes in v1:
time: 74.3 us; the launch traced here: 74 us
  Pallas kernels  64.5 us (87%)
  between operations  5.42 us (7%)
  local copies, waits for them, and re-layouts  4.13 us (6%)
    pallas_call x1, Pallas kernels, body(): pl.pallas_call(functools.partial(kernel, n_seg, n_tile, 1.0 / cells, 1.0...  64.5 us
    unnamed x7, local copies, waits for them, and re-layouts  4.13 us

profile of v1, /device:TPU:0, one launch (start us, length us, event | category | flops | bytes accessed | tf_op | source)
XLA Modules:
  0.0 74.0 jit_solution(7325674296214539694)
XLA Ops:
  1.9 0.0 copy-start
  1.9 1.2 %copy-done = f32[1,2,32,4096]{3,2,1,0:T(8,128)S(1)} copy-done((f32[1,2,32,4096]{3,2,1,0:T(8,128)S(1)}, f32[1,2,32,4096]{3,2,1,0:T(8,128)}, u32[]{:S(2)}) %copy-start) | copy-done | bytes 1048600
  3.1 0.0 copy-start.1
  3.1 1.2 %copy-done.1 = f32[1,2,32,4096]{3,2,1,0:T(8,128)S(1)} copy-done((f32[1,2,32,4096]{3,2,1,0:T(8,128)S(1)}, f32[1,2,32,4096]{3,2,1,0:T(8,128)}, u32[]{:S(2)}) %copy-start.1) | copy-done | bytes 1048600
  4.4 0.0 copy-start.2
  4.4 0.7 copy-done.2
  5.1 64.5 %shard_map.76 = (f32[1,2,32,4096]{3,2,1,0:T(8,128)S(1)}, f32[1]{0:T(128)}, f32[1]{0:T(128)}) custom-call(f32[1,2,32,4096]{3,2,1,0:T(8,128)S(1)} %copy-done, f32[1,2,32,4096]{3,2,1,0:T(8,128)S(1)} %copy-done.1, f32[1]{0:T(128)S(6)} %copy.11.time_ref, f32[1]{0:T(128)S(6)} %copy.12.change_ref, f32[1,4096]{1,0:T(1,128)S(1)} %copy-done.2), custom_call_target="tpu_custom_call" | custom-call | tf_op jit(solution)/shard_map/pallas_call | solution.py:292
  69.6 1.0 %copy.13 = f32[1,2,32,4096]{3,2,1,0:T(8,128)} copy(f32[1,2,32,4096]{3,2,1,0:T(8,128)S(1)} %get-tuple-element.6) | data formatting | bytes 2097152
Async XLA Ops:
  1.9 1.2 %copy-start = (f32[1,2,32,4096]{3,2,1,0:T(8,128)S(1)}, f32[1,2,32,4096]{3,2,1,0:T(8,128)}, u32[]{:S(2)}) copy-start(f32[1,2,32,4096]{3,2,1,0:T(8,128)} %base_hbm.1) | copy-start | bytes 3145732
  3.1 1.2 %copy-start.1 = (f32[1,2,32,4096]{3,2,1,0:T(8,128)S(1)}, f32[1,2,32,4096]{3,2,1,0:T(8,128)}, u32[]{:S(2)}) copy-start(f32[1,2,32,4096]{3,2,1,0:T(8,128)} %pert_hbm.1) | copy-start | bytes 3145732
  4.4 0.7 copy-start.2

commit v2 on v1

--- a/solution.py
+++ b/solution.py
@@ -87,9 +87,9 @@
 
 def kernel(
     n_seg, n_tile, scale_time, scale_square,
-    base_hbm, pert_hbm, time_ref, change_ref, force_ref,
+    base_hbm, pert_hbm, time_ref, change_ref, force_hbm,
     grad_ref, step_ref, square_ref,
-    base, pert, mid, pone, res, adj, rate0, rate1, image, ahead, behind, sums, pair, slots,
+    base, pert, mid, pone, res, adj, rate0, rate1, image, ahead, behind, sums, pair, slots, force_ref,
     local_sem, edge_send, edge_recv, ahead_send, ahead_recv, behind_send, behind_recv,
     pair_sem, slot_send, slot_recv,
 ):
@@ -111,6 +111,7 @@
     own = pl.ds(SUB, rows)
     loads = [
         pltpu.make_async_copy(base_hbm.at[0], base.at[:, own, :], local_sem.at[0]),
+        pltpu.make_async_copy(force_hbm, force_ref, local_sem.at[2]),
         pltpu.make_async_copy(pert_hbm.at[0], pert.at[:, own, :], local_sem.at[1]),
     ]
     for copy in loads:
@@ -119,20 +120,20 @@
 
     def edges(first, last, field, at):
         down = pltpu.make_async_remote_copy(
-            src_ref=last, dst_ref=field.at[:, pl.ds(0, SUB), :], send_sem=edge_send.at[at], recv_sem=edge_recv.at[at],
+            src_ref=last, dst_ref=field.at[:, pl.ds(SUB - 1, 1), :], send_sem=edge_send.at[at], recv_sem=edge_recv.at[at],
             device_id={"tile": tile_next}, device_id_type=MESH)
         up = pltpu.make_async_remote_copy(
-            src_ref=first, dst_ref=field.at[:, pl.ds(SUB + rows, SUB), :], send_sem=edge_send.at[at + 1],
+            src_ref=first, dst_ref=field.at[:, pl.ds(SUB + rows, 1), :], send_sem=edge_send.at[at + 1],
             recv_sem=edge_recv.at[at + 1], device_id={"tile": tile_prev}, device_id_type=MESH)
         down.start()
         up.start()
         return [down, up]
 
     def field_edges(field, at):
-        return edges(field.at[:, pl.ds(SUB, SUB), :], field.at[:, pl.ds(rows, SUB), :], field, at)
+        return edges(field.at[:, pl.ds(SUB, 1), :], field.at[:, pl.ds(SUB + rows - 1, 1), :], field, at)
 
     def hbm_edges(field_hbm, field, at):
-        return edges(field_hbm.at[0, :, pl.ds(0, SUB), :], field_hbm.at[0, :, pl.ds(rows - SUB, SUB), :], field, at)
+        return edges(field_hbm.at[0, :, pl.ds(0, 1), :], field_hbm.at[0, :, pl.ds(rows - 1, 1), :], field, at)
 
     pending = hbm_edges(base_hbm, base, 0) + hbm_edges(pert_hbm, pert, 2)
     aheads = []
@@ -141,7 +142,8 @@
         copy = pltpu.make_async_remote_copy(
             src_ref=pert_hbm.at[0, :, part, :], dst_ref=ahead.at[:, part, :], send_sem=ahead_send.at[k],
             recv_sem=ahead_recv.at[k], device_id={"seg": seg_prev}, device_id_type=MESH)
-        copy.start()
+        if k < blocks // 2:
+            copy.start()
         aheads.append(copy)
 
     def sweep(step):
@@ -167,7 +169,10 @@
             pone[c, own, pl.ds(col, chunk)] = images[c]
 
     sweep(first_step)
-    for copy in field_edges(mid, 4) + field_edges(pone, 6):
+    pending = field_edges(mid, 4) + field_edges(pone, 6)
+    for copy in aheads[blocks // 2 :]:
+        copy.start()
+    for copy in pending:
         copy.wait()
 
     def second_step(col):
@@ -179,16 +184,14 @@
             image[c, :, pl.ds(col, chunk)] = images[c]
 
     sweep(second_step)
-    for copy in aheads:
-        copy.wait_send()
     behinds = []
     for k in range(blocks):
         part = pl.ds(k * SUB, SUB)
         copy = pltpu.make_async_remote_copy(
             src_ref=image.at[:, part, :], dst_ref=behind.at[:, part, :], send_sem=behind_send.at[k],
             recv_sem=behind_recv.at[k], device_id={"seg": seg_next}, device_id_type=MESH)
-        copy.start()
         behinds.append(copy)
+    behinds[0].start()
 
     for k in range(blocks):
         aheads[k].wait_recv()
@@ -202,8 +205,14 @@
                 sums[1] += folded(rate1[c, part, pl.ds(col, chunk)] * value)
 
         sweep(residual_step)
-    for copy in field_edges(res, 8):
-        copy.wait()
+    pending = field_edges(res, 8)
+    quarter = max(blocks // 4, 1)
+    for copy in behinds[1 : 2 * quarter]:
+        copy.start()
+    for copy in pending + aheads:
+        copy.wait_send()
+    for copy in pending:
+        copy.wait_recv()
 
     def adjoint_one(col):
         outs = adjoint(windows(mid, col, chunk), windows(res, col, chunk), substep)
@@ -220,15 +229,10 @@
             device_id={"tile": lax.rem(tile + k, n_tile)}, device_id_type=MESH)
         copy.start()
         shares.append(copy)
+    for copy in behinds[2 * quarter : 3 * quarter]:
+        copy.start()
     for copy in pending:
         copy.wait()
-
-    def adjoint_zero(col):
-        outs = adjoint(windows(base, col, chunk), windows(adj, col, chunk), substep)
-        for c in range(2):
-            pone[c, own, pl.ds(col, chunk)] = outs[c] + pert[c, own, pl.ds(col, chunk)]
-
-    sweep(adjoint_zero)
 
     for copy in shares:
         copy.wait_send()
@@ -249,6 +253,16 @@
             device_id={"seg": lax.rem(seg + k, n_seg)}, device_id_type=MESH)
         copy.start()
         sends.append(copy)
+    for copy in behinds[3 * quarter :]:
+        copy.start()
+
+    def adjoint_zero(col):
+        outs = adjoint(windows(base, col, chunk), windows(adj, col, chunk), substep)
+        for c in range(2):
+            pone[c, own, pl.ds(col, chunk)] = outs[c] + pert[c, own, pl.ds(col, chunk)]
+
+    sweep(adjoint_zero)
+
     for copy in sends:
         copy.wait_send()
     for k in range(1, n_seg):
@@ -285,24 +299,25 @@
     plain = pltpu.VMEM((comps, rows, width), jnp.float32)
     part = (2, SUB, LANES)
     dma = pltpu.SemaphoreType.DMA
-    anywhere = pl.BlockSpec(memory_space=pl.ANY)
+    held = pl.BlockSpec(memory_space=pltpu.HBM)
     scalar = pl.BlockSpec(memory_space=pltpu.SMEM)
     vector = pl.BlockSpec(memory_space=pltpu.VMEM)
     one = jax.ShapeDtypeStruct((1,), jnp.float32)
     return pl.pallas_call(
         functools.partial(kernel, n_seg, n_tile, 1.0 / cells, 1.0 / (2 * cells)),
         out_shape=(jax.ShapeDtypeStruct(base.shape, jnp.float32), one, one),
-        in_specs=[anywhere, anywhere, scalar, scalar, vector],
+        in_specs=[held, held, scalar, scalar, held],
         out_specs=(vector, scalar, scalar),
         scratch_shapes=[wide] * 6 + [plain] * 5 + [
             pltpu.VMEM(part, jnp.float32),
             pltpu.VMEM((n_tile, *part), jnp.float32),
             pltpu.VMEM((n_seg, *part), jnp.float32),
-            dma((2,)), dma((12,)), dma((12,)), dma((blocks,)), dma((blocks,)), dma((blocks,)), dma((blocks,)),
+            pltpu.VMEM((1, width), jnp.float32),
+            dma((3,)), dma((12,)), dma((12,)), dma((blocks,)), dma((blocks,)), dma((blocks,)), dma((blocks,)),
             dma((2, n_tile)), dma((n_seg,)), dma((n_seg,)),
         ],
         compiler_params=pltpu.CompilerParams(
-            collective_id=0, has_side_effects=True, vmem_limit_bytes=40 * 1024 * 1024
+            collective_id=0, has_side_effects=True, vmem_limit_bytes=62 * 1024 * 1024
         ),
     )(base, direction, step_time, step_change, forcing)
 

time: 74.3 us -> 68.9 us (0.927)
  the two profiles are of different devices: /device:TPU:0 before, /device:TPU:12 now
where the time goes in v2:
time: 68.9 us; the launch traced here: 68.7 us
  Pallas kernels  61 us (89%)
  between operations  5.38 us (8%)
  local copies, waits for them, and re-layouts  2.27 us (3%)
    pallas_call x1, Pallas kernels, body(): pl.pallas_call(functools.partial(kernel, n_seg, n_tile, 1.0 / cells, 1.0...  61 us
    unnamed x1, local copies, waits for them, and re-layouts  2.27 us

profile of v2, /device:TPU:12, one launch (start us, length us, event | category | flops | bytes accessed | tf_op | source)
XLA Modules:
  0.0 68.7 jit_solution(3734122440133296119)
XLA Ops:
  1.9 61.0 %shard_map.76 = (f32[1,2,32,4096]{3,2,1,0:T(8,128)}, f32[1]{0:T(128)}, f32[1]{0:T(128)}) custom-call(f32[1,2,32,4096]{3,2,1,0:T(8,128)} %base_hbm.1, f32[1,2,32,4096]{3,2,1,0:T(8,128)} %pert_hbm.1, f32[1]{0:T(128)S(6)} %copy.11.time_ref, f32[1]{0:T(128)S(6)} %copy.12.change_ref, f32[1,4096]{1,0:T(1,128)} %constant.2.clone.force_hbm), custom_call_target="tpu_custom_call" | custom-call | tf_op jit(solution)/shard_map/pallas_call | solution.py:306
  62.9 2.3 %copy.13 = f32[1,2,32,4096]{3,2,1,0:T(8,128)} copy(f32[1,2,32,4096]{3,2,1,0:T(8,128)} %get-tuple-element.6) | data formatting | bytes 2097152

commit v3 on v2

--- a/solution.py
+++ b/solution.py
@@ -191,7 +191,6 @@
             src_ref=image.at[:, part, :], dst_ref=behind.at[:, part, :], send_sem=behind_send.at[k],
             recv_sem=behind_recv.at[k], device_id={"seg": seg_next}, device_id_type=MESH)
         behinds.append(copy)
-    behinds[0].start()
 
     for k in range(blocks):
         aheads[k].wait_recv()
@@ -207,7 +206,7 @@
         sweep(residual_step)
     pending = field_edges(res, 8)
     quarter = max(blocks // 4, 1)
-    for copy in behinds[1 : 2 * quarter]:
+    for copy in behinds[: 2 * quarter]:
         copy.start()
     for copy in pending + aheads:
         copy.wait_send()

time: 68.9 us -> 67 us (0.972)
  the two profiles are of different devices: /device:TPU:12 before, /device:TPU:0 now
where the time goes in v3:
time: 67 us; the launch traced here: 66.8 us
  Pallas kernels  59.1 us (88%)
  between operations  5.38 us (8%)
  local copies, waits for them, and re-layouts  2.27 us (3%)
    pallas_call x1, Pallas kernels, body(): pl.pallas_call(functools.partial(kernel, n_seg, n_tile, 1.0 / cells, 1.0...  59.1 us
    unnamed x1, local copies, waits for them, and re-layouts  2.27 us

profile of v3, /device:TPU:0, one launch (start us, length us, event | category | flops | bytes accessed | tf_op | source)
XLA Modules:
  0.0 66.8 jit_solution(9755918775044912137)
XLA Ops:
  1.9 59.1 %shard_map.76 = (f32[1,2,32,4096]{3,2,1,0:T(8,128)}, f32[1]{0:T(128)}, f32[1]{0:T(128)}) custom-call(f32[1,2,32,4096]{3,2,1,0:T(8,128)} %base_hbm.1, f32[1,2,32,4096]{3,2,1,0:T(8,128)} %pert_hbm.1, f32[1]{0:T(128)S(6)} %copy.11.time_ref, f32[1]{0:T(128)S(6)} %copy.12.change_ref, f32[1,4096]{1,0:T(1,128)} %constant.2.clone.force_hbm), custom_call_target="tpu_custom_call" | custom-call | tf_op jit(solution)/shard_map/pallas_call | solution.py:305
  61.1 2.3 %copy.13 = f32[1,2,32,4096]{3,2,1,0:T(8,128)} copy(f32[1,2,32,4096]{3,2,1,0:T(8,128)} %get-tuple-element.6) | data formatting | bytes 2097152
